TPU v7x, 32 devices: a whole 2x2x4 slice. The times are simulated.
32 devices in a mesh: dp: 8 (over z, x), seq: 4 (over y, core).
Axes of the slice: x: 2, y: 2, z: 4, core: 2. Of those that a mesh axis runs over, the one named last changes fastest.
Arguments:
- hidden_in: bfloat16 [24576, 1024], P(('dp', 'seq')), may hold values from -6 to 6
- key_bias: float32 [8, 3072], P('dp', 'seq'), may hold values from -4 to 4
- w_qkv: bfloat16 [1024, 3072], P('dp'), may hold values from -0.1875 to 0.1875
- bias_q: bfloat16 [1024], P('dp'), may hold values from -3 to 3
- bias_v: bfloat16 [1024], P('dp'), may hold values from -0.75 to 0.75
- w_out: bfloat16 [1024, 1024], P('dp'), may hold values from -3 to 3
- bias_out: bfloat16 [1024], P('dp'), may hold values from -3 to 3
- gain_attn: bfloat16 [1024], P('dp'), may hold values from 0.25 to 1.75
- shift_attn: bfloat16 [1024], P('dp'), may hold values from -3 to 3
- w_up: bfloat16 [1024, 4096], P('dp'), may hold values from -0.1875 to 0.1875
- bias_up: bfloat16 [4096], P('dp'), may hold values from -3 to 3
- w_down: bfloat16 [4096, 1024], P('dp'), may hold values from -0.09375 to 0.09375
- bias_down: bfloat16 [1024], P('dp'), may hold values from -3 to 3
- gain_ffn: bfloat16 [1024], P('dp'), may hold values from 0.25 to 1.75
- shift_ffn: bfloat16 [1024], P('dp'), may hold values from -3 to 3
- grad_out: bfloat16 [24576, 1024], P(('dp', 'seq')), may hold values from -6 to 6
Outputs:
- output: bfloat16 [24576, 1024], P(('dp', 'seq'))
- grad_in: float32 [24576, 1024], P(('dp', 'seq'))
- grad_w_qkv: float32 [1024, 3072], P('dp')
- grad_bias_q: float32 [1024], P('dp')
- grad_bias_v: float32 [1024], P('dp')
- grad_w_out: float32 [1024, 1024], P('dp')
- grad_bias_out: float32 [1024], P('dp')
- grad_gain_attn: float32 [1024], P('dp')
- grad_shift_attn: float32 [1024], P('dp')
- grad_w_up: float32 [1024, 4096], P('dp')
- grad_bias_up: float32 [4096], P('dp')
- grad_w_down: float32 [4096, 1024], P('dp')
- grad_bias_down: float32 [1024], P('dp')
- grad_gain_ffn: float32 [1024], P('dp')
- grad_shift_ffn: float32 [1024], P('dp')
All inputs are finite; a program needn't handle non-finite values.
Results may differ from a plain program's by a relative error of at most 0.02.
Values may be sent and summed in bfloat16 or wider, within the bound.
A program may use at most 192 MiB of HBM per device.

v0:
```python
import jax
import jax.numpy as jnp
from jax import lax
from jax.sharding import PartitionSpec as P

HEAD_DIM = 64
norm_eps = 1e-05


def shortened(array):

    def short(part):
        return part.astype(jnp.bfloat16) if part.dtype == jnp.float32 else part

    return jax.tree.map(short, array)


def layer_norm(hidden, gain_vec, shift_vec):
    row_mean = jnp.mean(hidden, -1, keepdims=True)
    centered = hidden - row_mean
    row_var = jnp.mean(centered * centered, -1, keepdims=True)
    return centered * lax.rsqrt(row_var + norm_eps) * gain_vec + shift_vec


def gelu_exact(pre_act):
    return jax.nn.gelu(pre_act, approximate=False)


def matmul(left, right):
    return jnp.dot(left, right, preferred_element_type=jnp.float32)


def matmul_left(left, right):
    return lax.dot_general(
        left, right, (((0,), (0,)), ((), ())), preferred_element_type=jnp.float32
    )


def matmul_right(left, right):
    return lax.dot_general(
        left, right, (((1,), (1,)), ((), ())), preferred_element_type=jnp.float32
    )


def attend_forward(queries, keys_all, values_all, bias_row, score_scale):
    length, heads_loc, head_width = queries.shape
    block_rows = min(512, length)
    head_step = min(2, heads_loc)
    blocks = queries.reshape(length // block_rows, block_rows, heads_loc, head_width)

    def one_block(query_blk):
        pieces = []
        totals_list = []
        for start_head in range(0, heads_loc, head_step):
            part = slice(start_head, start_head + head_step)
            scores = (
                jnp.einsum(
                    "bhe,lhe->hbl",
                    query_blk[:, part],
                    keys_all[:, part],
                    preferred_element_type=jnp.float32,
                )
                * score_scale
                + bias_row
            )
            row_max = jnp.max(scores, -1, keepdims=True)
            expo = jnp.exp(scores - row_max)
            row_total = jnp.sum(expo, -1, keepdims=True)
            probs_low = (expo / row_total).astype(jnp.bfloat16)
            pieces.append(
                jnp.einsum(
                    "hbl,lhe->bhe",
                    probs_low,
                    values_all[:, part],
                    preferred_element_type=jnp.float32,
                )
            )
            totals_list.append((row_max + jnp.log(row_total))[..., 0])
        return (jnp.concatenate(pieces, 1).astype(jnp.bfloat16), jnp.concatenate(totals_list, 0))

    context, log_total = lax.map(one_block, blocks)
    return (context.reshape(length, heads_loc * head_width), log_total)


def attend_backward(queries, keys_all, values_all, bias_row, score_scale, log_total, context_grad):
    length, heads_loc, head_width = queries.shape
    block_rows = min(512, length)
    head_step = min(2, heads_loc)
    query_blocks = queries.reshape(length // block_rows, block_rows, heads_loc, head_width)
    grad_blocks = context_grad.reshape(length // block_rows, block_rows, heads_loc, head_width)

    def one_block(carry_in, item_in):
        key_acc, value_acc = carry_in
        query_blk, grad_blk, total_blk = item_in
        query_parts = []
        key_parts = []
        value_parts = []
        for start_head in range(0, heads_loc, head_step):
            part = slice(start_head, start_head + head_step)
            scores = (
                jnp.einsum(
                    "bhe,lhe->hbl",
                    query_blk[:, part],
                    keys_all[:, part],
                    preferred_element_type=jnp.float32,
                )
                * score_scale
                + bias_row
            )
            probs_full = jnp.exp(scores - total_blk[part][..., None])
            d_probs = jnp.einsum(
                "bhe,lhe->hbl",
                grad_blk[:, part],
                values_all[:, part],
                preferred_element_type=jnp.float32,
            )
            row_dot = jnp.sum(probs_full * d_probs, -1, keepdims=True)
            d_scores = (probs_full * (d_probs - row_dot)).astype(jnp.bfloat16)
            query_parts.append(
                jnp.einsum(
                    "hbl,lhe->bhe", d_scores, keys_all[:, part], preferred_element_type=jnp.float32
                )
                * score_scale
            )
            key_parts.append(
                jnp.einsum(
                    "hbl,bhe->lhe", d_scores, query_blk[:, part], preferred_element_type=jnp.float32
                )
                * score_scale
            )
            value_parts.append(
                jnp.einsum(
                    "hbl,bhe->lhe",
                    probs_full.astype(jnp.bfloat16),
                    grad_blk[:, part],
                    preferred_element_type=jnp.float32,
                )
            )
        key_acc = key_acc + jnp.concatenate(key_parts, 1)
        value_acc = value_acc + jnp.concatenate(value_parts, 1)
        return ((key_acc, value_acc), jnp.concatenate(query_parts, 1))

    empty = jnp.zeros((length, heads_loc, head_width), jnp.float32)
    (key_grad, value_grad), query_grad = lax.scan(
        one_block, (empty, empty), (query_blocks, grad_blocks, log_total)
    )
    return (query_grad.reshape(length, heads_loc, head_width), key_grad, value_grad)


def local(
    hidden_in,
    key_bias,
    w_qkv,
    bias_q,
    bias_v,
    w_out,
    bias_out,
    gain_attn,
    shift_attn,
    w_up,
    bias_up,
    w_down,
    bias_down,
    gain_ffn,
    shift_ffn,
    grad_out,
):
    groups = lax.axis_size("seq")
    params = (
        lax.all_gather(w_qkv, "dp", axis=0, tiled=True),
        lax.all_gather(bias_q, "dp", axis=0, tiled=True),
        lax.all_gather(bias_v, "dp", axis=0, tiled=True),
        lax.all_gather(w_out, "dp", axis=0, tiled=True),
        lax.all_gather(bias_out, "dp", axis=0, tiled=True),
        lax.all_gather(gain_attn, "dp", axis=0, tiled=True),
        lax.all_gather(shift_attn, "dp", axis=0, tiled=True),
        lax.all_gather(w_up, "dp", axis=0, tiled=True),
        lax.all_gather(bias_up, "dp", axis=0, tiled=True),
        lax.all_gather(w_down, "dp", axis=0, tiled=True),
        lax.all_gather(bias_down, "dp", axis=0, tiled=True),
        lax.all_gather(gain_ffn, "dp", axis=0, tiled=True),
        lax.all_gather(shift_ffn, "dp", axis=0, tiled=True),
    )
    full_bias_q = params[1].astype(jnp.float32)
    full_bias_v = params[2].astype(jnp.float32)
    full_bias_out = params[4].astype(jnp.float32)
    full_gain_attn = params[5].astype(jnp.float32)
    full_shift_attn = params[6].astype(jnp.float32)
    full_bias_up = params[8].astype(jnp.float32)
    full_bias_down = params[10].astype(jnp.float32)
    full_gain_ffn = params[11].astype(jnp.float32)
    full_shift_ffn = params[12].astype(jnp.float32)
    tok_rows, model_width = hidden_in.shape
    group_width = model_width // groups
    heads_loc = group_width // HEAD_DIM
    score_scale = HEAD_DIM ** (-0.5)
    no_bias = jnp.zeros((model_width,), jnp.float32)
    qkv_rows = matmul(hidden_in, params[0]) + jnp.concatenate([full_bias_q, no_bias, full_bias_v])
    qkv_rows = qkv_rows.astype(jnp.bfloat16).reshape(tok_rows, 3, groups, group_width)
    heads_in = lax.all_to_all(qkv_rows, "seq", split_axis=2, concat_axis=0, tiled=True)
    length = heads_in.shape[0]
    queries = heads_in[:, 0, 0].reshape(length, heads_loc, HEAD_DIM)
    keys_all = heads_in[:, 1, 0].reshape(length, heads_loc, HEAD_DIM)
    values_all = heads_in[:, 2, 0].reshape(length, heads_loc, HEAD_DIM)
    bias_row = lax.all_gather(key_bias, "seq", axis=1, tiled=True)[0]
    context_heads, log_total = attend_forward(queries, keys_all, values_all, bias_row, score_scale)
    context = lax.all_to_all(
        shortened(context_heads.reshape(length, 1, group_width)),
        "seq",
        split_axis=0,
        concat_axis=1,
        tiled=True,
    ).reshape(tok_rows, model_width)
    attended = hidden_in.astype(jnp.float32) + matmul(context, params[3]) + full_bias_out
    normed = layer_norm(attended, full_gain_attn, full_shift_attn)
    normed_low = normed.astype(jnp.bfloat16)
    pre_act = matmul(normed_low, params[7]) + full_bias_up
    activ = gelu_exact(pre_act).astype(jnp.bfloat16)
    branch_sum = normed + matmul(activ, params[9]) + full_bias_down
    output = layer_norm(branch_sum, full_gain_ffn, full_shift_ffn).astype(jnp.bfloat16)
    matrices = (
        lax.all_gather(w_qkv, "dp", axis=0, tiled=True),
        lax.all_gather(w_out, "dp", axis=0, tiled=True),
        lax.all_gather(w_up, "dp", axis=0, tiled=True),
        lax.all_gather(w_down, "dp", axis=0, tiled=True),
    )
    upstream = grad_out.astype(jnp.float32)
    _, norm_back = jax.vjp(layer_norm, branch_sum, full_gain_ffn, full_shift_ffn)
    d_branch, grad_gain_ffn, grad_shift_ffn = norm_back(upstream)
    grad_bias_down = jnp.sum(d_branch, 0)
    d_branch_low = d_branch.astype(jnp.bfloat16)
    grad_w_down = matmul_left(activ, d_branch_low)
    d_activ = matmul_right(d_branch_low, matrices[3])
    _, gelu_back = jax.vjp(gelu_exact, pre_act)
    d_pre = gelu_back(d_activ)[0]
    grad_bias_up = jnp.sum(d_pre, 0)
    d_pre_low = d_pre.astype(jnp.bfloat16)
    grad_w_up = matmul_left(normed_low, d_pre_low)
    d_normed = d_branch + matmul_right(d_pre_low, matrices[2])
    _, attn_norm_back = jax.vjp(layer_norm, attended, full_gain_attn, full_shift_attn)
    d_attended, grad_gain_attn, grad_shift_attn = attn_norm_back(d_normed)
    grad_bias_out = jnp.sum(d_attended, 0)
    d_attended_low = d_attended.astype(jnp.bfloat16)
    grad_w_out = matmul_left(context, d_attended_low)
    d_context = matmul_right(d_attended_low, matrices[1]).astype(jnp.bfloat16)
    d_context_heads = lax.all_to_all(
        d_context.reshape(tok_rows, groups, group_width),
        "seq",
        split_axis=1,
        concat_axis=0,
        tiled=True,
    )
    query_grad, key_grad, value_grad = attend_backward(
        queries,
        keys_all,
        values_all,
        bias_row,
        score_scale,
        log_total,
        d_context_heads.reshape(length, heads_loc, HEAD_DIM),
    )
    d_heads = (
        jnp.stack([query_grad, key_grad, value_grad], 1)
        .astype(jnp.bfloat16)
        .reshape(length, 3, 1, group_width)
    )
    d_qkv = lax.all_to_all(d_heads, "seq", split_axis=0, concat_axis=2, tiled=True).reshape(
        tok_rows, 3 * model_width
    )
    grad_bias_q = jnp.sum(d_qkv[:, :model_width].astype(jnp.float32), 0)
    grad_bias_v = jnp.sum(d_qkv[:, 2 * model_width :].astype(jnp.float32), 0)
    grad_w_qkv = matmul_left(hidden_in, d_qkv)
    grad_in = d_attended + matmul_right(d_qkv, matrices[0])
    local_grads = (
        grad_w_qkv,
        grad_bias_q,
        grad_bias_v,
        grad_w_out,
        grad_bias_out,
        grad_gain_attn,
        grad_shift_attn,
        grad_w_up,
        grad_bias_up,
        grad_w_down,
        grad_bias_down,
        grad_gain_ffn,
        grad_shift_ffn,
    )
    shares = (
        lax.psum_scatter(
            local_grads[0].astype(jnp.bfloat16), "dp", scatter_dimension=0, tiled=True
        ).astype(jnp.float32),
        lax.psum_scatter(
            local_grads[1].astype(jnp.bfloat16), "dp", scatter_dimension=0, tiled=True
        ).astype(jnp.float32),
        lax.psum_scatter(
            local_grads[2].astype(jnp.bfloat16), "dp", scatter_dimension=0, tiled=True
        ).astype(jnp.float32),
        lax.psum_scatter(
            local_grads[3].astype(jnp.bfloat16), "dp", scatter_dimension=0, tiled=True
        ).astype(jnp.float32),
        lax.psum_scatter(
            local_grads[4].astype(jnp.bfloat16), "dp", scatter_dimension=0, tiled=True
        ).astype(jnp.float32),
        lax.psum_scatter(
            local_grads[5].astype(jnp.bfloat16), "dp", scatter_dimension=0, tiled=True
        ).astype(jnp.float32),
        lax.psum_scatter(
            local_grads[6].astype(jnp.bfloat16), "dp", scatter_dimension=0, tiled=True
        ).astype(jnp.float32),
        lax.psum_scatter(
            local_grads[7].astype(jnp.bfloat16), "dp", scatter_dimension=0, tiled=True
        ).astype(jnp.float32),
        lax.psum_scatter(
            local_grads[8].astype(jnp.bfloat16), "dp", scatter_dimension=0, tiled=True
        ).astype(jnp.float32),
        lax.psum_scatter(
            local_grads[9].astype(jnp.bfloat16), "dp", scatter_dimension=0, tiled=True
        ).astype(jnp.float32),
        lax.psum_scatter(
            local_grads[10].astype(jnp.bfloat16), "dp", scatter_dimension=0, tiled=True
        ).astype(jnp.float32),
        lax.psum_scatter(
            local_grads[11].astype(jnp.bfloat16), "dp", scatter_dimension=0, tiled=True
        ).astype(jnp.float32),
        lax.psum_scatter(
            local_grads[12].astype(jnp.bfloat16), "dp", scatter_dimension=0, tiled=True
        ).astype(jnp.float32),
    )
    owned_grads = (
        lax.psum(shares[0].astype(jnp.bfloat16), "seq").astype(jnp.float32),
        lax.psum(shares[1].astype(jnp.bfloat16), "seq").astype(jnp.float32),
        lax.psum(shares[2].astype(jnp.bfloat16), "seq").astype(jnp.float32),
        lax.psum(shares[3].astype(jnp.bfloat16), "seq").astype(jnp.float32),
        lax.psum(shares[4].astype(jnp.bfloat16), "seq").astype(jnp.float32),
        lax.psum(shares[5].astype(jnp.bfloat16), "seq").astype(jnp.float32),
        lax.psum(shares[6].astype(jnp.bfloat16), "seq").astype(jnp.float32),
        lax.psum(shares[7].astype(jnp.bfloat16), "seq").astype(jnp.float32),
        lax.psum(shares[8].astype(jnp.bfloat16), "seq").astype(jnp.float32),
        lax.psum(shares[9].astype(jnp.bfloat16), "seq").astype(jnp.float32),
        lax.psum(shares[10].astype(jnp.bfloat16), "seq").astype(jnp.float32),
        lax.psum(shares[11].astype(jnp.bfloat16), "seq").astype(jnp.float32),
        lax.psum(shares[12].astype(jnp.bfloat16), "seq").astype(jnp.float32),
    )
    return (
        output,
        grad_in,
        owned_grads[0],
        owned_grads[1],
        owned_grads[2],
        owned_grads[3],
        owned_grads[4],
        owned_grads[5],
        owned_grads[6],
        owned_grads[7],
        owned_grads[8],
        owned_grads[9],
        owned_grads[10],
        owned_grads[11],
        owned_grads[12],
    )


def solution(mesh):
    return jax.shard_map(
        local,
        mesh=mesh,
        in_specs=(
            P(("dp", "seq"), None),
            P("dp", "seq"),
            P("dp", None),
            P("dp"),
            P("dp"),
            P("dp", None),
            P("dp"),
            P("dp"),
            P("dp"),
            P("dp", None),
            P("dp"),
            P("dp", None),
            P("dp"),
            P("dp"),
            P("dp"),
            P(("dp", "seq"), None),
        ),
        out_specs=(
            P(("dp", "seq"), None),
            P(("dp", "seq"), None),
            P("dp", None),
            P("dp"),
            P("dp"),
            P("dp", None),
            P("dp"),
            P("dp"),
            P("dp"),
            P("dp", None),
            P("dp"),
            P("dp", None),
            P("dp"),
            P("dp"),
            P("dp"),
        ),
        check_vma=False,
    )
```

profile of v0, /device:TPU:0, one launch (start us, length us, event | category | flops | bytes accessed | tf_op | source)
XLA Modules:
  0.0 1988.5 jit_solution(5152587531738367793)
XLA Ops:
  9.4 22.5 %all-gather.1 = bf16[8,1,128]{2,1,0:T(2,128)(2,1)S(1)} all-gather(bf16[1,1,128]{2,1,0:T(2,128)(2,1)} %bitcast.231), channel_id=1, replica_groups=mesh['dp'=8,'seq'=4] {'dp'}, dimensions={0}, use_global_device_ids=true | all-gather | bytes 2304 | tf_op jit(solution)/shard_map/all_gather | solution.py:172
  31.9 16.7 all-gather
  48.6 63.4 %all-gather.14.cloned.1.call-done = bf16[1024,3072]{1,0:T(8,128)(2,1)} async-done(((bf16[128,3072]{1,0:T(8,128)(2,1)}), bf16[1024,3072]{1,0:T(8,128)(2,1)}) %all-gather.14.cloned.1.call-update) | async-done | bytes 6291472 | tf_op jit(solution)/shard_map/all_gather | solution.py:170
  112.0 9.1 add_convert_fusion
  121.1 9.7 reshape.215
  141.7 54.1 %all_gather.49 = f32[1,3072]{1,0:T(1,128)S(1)} all-gather(f32[1,768]{1,0:T(1,128)S(1)} %copy-done.34), channel_id=1, replica_groups=mesh['dp'=8,'seq'=4] {'seq'}, dimensions={1}, use_global_device_ids=true | all-gather | bytes 15360 | tf_op jit(solution)/shard_map/all_gather | solution.py:205
  213.4 180.6 %while.27 = (s32[]{:T(128)}, bf16[6,512,4,64]{1,3,2,0:T(8,128)(2,1)}, f32[6,4,512]{2,1,0:T(4,128)S(1)}, bf16[6,512,4,64]{1,3,2,0:T(8,128)(2,1)}, bf16[3072,4,64]...) while((s32[]{:T(128)}, bf16[6,512,4,64]{1,3,2,0:T(8,128)(2,1)}, ...), condition=%wide.region_5.6_spmd, body=%wide.region_0.5_spmd.sunk | while | flops 1686765568 | bytes 80098904 | solution.py:81
  399.7 22.8 %reshape.246 = bf16[3072,1,256]{2,1,0:T(2,128)(2,1)} reshape(bf16[6,512,4,64]{3,2,1,0:T(4,128)(2,1)} %copy.114) | data formatting | bytes 3145728 | tf_op jit(solution)/shard_map/reshape;reshape | solution.py:208
  423.0 16.7 reduce.3
  445.9 17.5 all-gather.2
  463.3 16.9 all-gather.3
  480.2 17.5 all-gather.4
  497.7 26.0 %all-gather.5 = bf16[8,1,512]{2,1,0:T(2,128)(2,1)S(1)} all-gather(bf16[1,1,512]{2,1,0:T(2,128)(2,1)S(1)} %reshape.229), channel_id=1, replica_groups=mesh['dp'=8,'seq'=4] {'dp'}, dimensions={0}, use_global_device_ids=true | all-gather | bytes 9216 | tf_op jit(solution)/shard_map/all_gather | solution.py:178
  523.8 16.2 all-gather.6
  539.9 18.2 all-gather.7
  558.1 16.2 all-gather.8
  586.4 39.4 %multiply_convert_fusion.2 = (bf16[768,4096]{1,0:T(8,128)(2,1)}, f32[768,4096]{1,0:T(8,128)}, f32[768,4096]{1,0:T(8,128)}) fusion(f32[4096]{0:T(1024)S(1)} %bitcast.222, bf16[1024,4096]{1,0:T(8,128)(2,1)} %all-gather.18.cloned.1.call-done, f32[768,1024]{1,0:T(8,128)S(1)} %get-tuple-element.410, f32[1024]{0:T(1024)S(1)} %bitcast.226, ...), kind=kOutput, calls=%fused_computation.100 | convolution fusion | flops 6654001152 | bytes 43022336 | tf_op jit(solution)/shard_map/dot_general | solution.py:30
  625.8 11.7 fusion.105
  642.8 21.7 %fusion.106 = (bf16[4096]{0:T(1024)(128)(2,1)}, bf16[768,4096]{1,0:T(8,128)(2,1)}) fusion(f32[768,4096]{1,0:T(8,128)} %get-tuple-element.392, bf16[4096,1024]{1,0:T(8,128)(2,1)} %all-gather.20.cloned.1.call-done, f32[768,1024]{1,0:T(8,128)} %get-tuple-element.390, f32[768]{0:T(1024)S(1)} %negate_multiply_fusion.2, f32[768,4096]{1,0:T(8,128)} %get-tuple-element.411, ...), kind=kOutput, calls=%fused_computation.167 | convolution fusion | flops 6494351360 | bytes 43019264 | tf_op jit(solution)/shard_map/dot_general | solution.py:40
  664.5 13.4 multiply_reduce_fusion.2
  687.8 20.0 %all-to-all-done.2 = bf16[768,4,256]{0,2,1:T(8,128)(2,1)S(1)} async-done(((bf16[768,4,256]{0,2,1:T(8,128)(2,1)}), bf16[768,4,256]{0,2,1:T(8,128)(2,1)S(1)}, u32[]{:S(2)}, u32[]{:S(2)}) %all-to-all-start.2) | async-done | bytes 1572896 | tf_op jit(solution)/shard_map/all_to_all | solution.py:246
  717.6 568.6 %while.28 = (s32[]{:T(128)}, f32[3072,4,64]{0,2,1:T(8,128)}, f32[3072,4,64]{0,2,1:T(8,128)}, bf16[6,512,4,64]{1,3,2,0:T(8,128)(2,1)}, bf16[6,512,4,64]{1,3,2,0:T...) while((s32[]{:T(128)}, f32[3072,4,64]{0,2,1:T(8,128)}, ...), condition=%wide.region_17.18_spmd.clone, body=%wide.region_14.17_spmd.clone.sunk | while | flops 4127193088 | bytes 341160832 | solution.py:144
  740.8 20.1 %multiply_reduce_fusion.7 = (f32[2,512]{1,0:T(2,128)S(1)}, f32[2,512]{1,0:T(2,128)S(1)}, f32[2,512,3072]{2,1,0:T(8,128)}) fusion(f32[2,512,3072]{2,1,0:T(8,128)} %fusion.191, f32[2,512]{1,0:T(2,128)S(1)} %get-tuple-element.546, f32[3072]{0:T(1024)S(1)} %bitcast.204, f32[2,512,3072]{2,1,0:T(8,128)} %fusion.192, f32[2,512]{1,0:T(2,128)S(1)} %get-tuple-element.547, ...), kind=kOutput, calls=%fused_computation.39.clone.1 | convolution fusion | flops 434108416 | bytes 51409408 | tf_op jit(solution)/shard_map/while/body/eval_jaxpr/bhe,lhe->hbl/dot_general | solution.py:111
  760.9 17.9 multiply_convert_fusion.4
  834.0 20.1 %multiply_reduce_fusion.7 = (f32[2,512]{1,0:T(2,128)S(1)}, f32[2,512]{1,0:T(2,128)S(1)}, f32[2,512,3072]{2,1,0:T(8,128)}) fusion(f32[2,512,3072]{2,1,0:T(8,128)} %fusion.191, f32[2,512]{1,0:T(2,128)S(1)} %get-tuple-element.546, f32[3072]{0:T(1024)S(1)} %bitcast.204, f32[2,512,3072]{2,1,0:T(8,128)} %fusion.192, f32[2,512]{1,0:T(2,128)S(1)} %get-tuple-element.547, ...), kind=kOutput, calls=%fused_computation.39.clone.1 | convolution fusion | flops 434108416 | bytes 51409408 | tf_op jit(solution)/shard_map/while/body/eval_jaxpr/bhe,lhe->hbl/dot_general | solution.py:111
  854.0 17.9 multiply_convert_fusion.4
  897.1 8.8 maximum_add_fusion.3
  928.9 20.0 %multiply_reduce_fusion.7 = (f32[2,512]{1,0:T(2,128)S(1)}, f32[2,512]{1,0:T(2,128)S(1)}, f32[2,512,3072]{2,1,0:T(8,128)}) fusion(f32[2,512,3072]{2,1,0:T(8,128)} %fusion.191, f32[2,512]{1,0:T(2,128)S(1)} %get-tuple-element.546, f32[3072]{0:T(1024)S(1)} %bitcast.204, f32[2,512,3072]{2,1,0:T(8,128)} %fusion.192, f32[2,512]{1,0:T(2,128)S(1)} %get-tuple-element.547, ...), kind=kOutput, calls=%fused_computation.39.clone.1 | convolution fusion | flops 434108416 | bytes 51409408 | tf_op jit(solution)/shard_map/while/body/eval_jaxpr/bhe,lhe->hbl/dot_general | solution.py:111
  948.9 17.9 multiply_convert_fusion.4
  992.0 8.8 maximum_add_fusion.3
  1023.8 20.1 %multiply_reduce_fusion.7 = (f32[2,512]{1,0:T(2,128)S(1)}, f32[2,512]{1,0:T(2,128)S(1)}, f32[2,512,3072]{2,1,0:T(8,128)}) fusion(f32[2,512,3072]{2,1,0:T(8,128)} %fusion.191, f32[2,512]{1,0:T(2,128)S(1)} %get-tuple-element.546, f32[3072]{0:T(1024)S(1)} %bitcast.204, f32[2,512,3072]{2,1,0:T(8,128)} %fusion.192, f32[2,512]{1,0:T(2,128)S(1)} %get-tuple-element.547, ...), kind=kOutput, calls=%fused_computation.39.clone.1 | convolution fusion | flops 434108416 | bytes 51409408 | tf_op jit(solution)/shard_map/while/body/eval_jaxpr/bhe,lhe->hbl/dot_general | solution.py:111
  1043.9 17.9 multiply_convert_fusion.4
  1118.9 20.0 %multiply_reduce_fusion.7 = (f32[2,512]{1,0:T(2,128)S(1)}, f32[2,512]{1,0:T(2,128)S(1)}, f32[2,512,3072]{2,1,0:T(8,128)}) fusion(f32[2,512,3072]{2,1,0:T(8,128)} %fusion.191, f32[2,512]{1,0:T(2,128)S(1)} %get-tuple-element.546, f32[3072]{0:T(1024)S(1)} %bitcast.204, f32[2,512,3072]{2,1,0:T(8,128)} %fusion.192, f32[2,512]{1,0:T(2,128)S(1)} %get-tuple-element.547, ...), kind=kOutput, calls=%fused_computation.39.clone.1 | convolution fusion | flops 434108416 | bytes 51409408 | tf_op jit(solution)/shard_map/while/body/eval_jaxpr/bhe,lhe->hbl/dot_general | solution.py:111
  1138.9 17.9 multiply_convert_fusion.4
  1213.8 20.1 %multiply_reduce_fusion.7 = (f32[2,512]{1,0:T(2,128)S(1)}, f32[2,512]{1,0:T(2,128)S(1)}, f32[2,512,3072]{2,1,0:T(8,128)}) fusion(f32[2,512,3072]{2,1,0:T(8,128)} %fusion.191, f32[2,512]{1,0:T(2,128)S(1)} %get-tuple-element.546, f32[3072]{0:T(1024)S(1)} %bitcast.204, f32[2,512,3072]{2,1,0:T(8,128)} %fusion.192, f32[2,512]{1,0:T(2,128)S(1)} %get-tuple-element.547, ...), kind=kOutput, calls=%fused_computation.39.clone.1 | convolution fusion | flops 434108416 | bytes 51409408 | tf_op jit(solution)/shard_map/while/body/eval_jaxpr/bhe,lhe->hbl/dot_general | solution.py:111
  1233.9 17.9 multiply_convert_fusion.4
  1299.2 10.1 copy.110
  1309.3 74.6 %all_to_all.63 = bf16[3072,3,1,256]{3,1,2,0:T(4,128)(2,1)S(1)} all-to-all(bf16[3072,3,1,256]{3,1,2,0:T(4,128)(2,1)} %copy.110), channel_id=1, replica_groups=mesh['dp'=8,'seq'=4] {'seq'}, dimensions={0} | all-to-all | bytes 9437184 | tf_op jit(solution)/shard_map/all_to_all | solution.py:267
  1393.5 9.3 convert_bitcast_fusion
  1418.1 12.5 convolution_convert_fusion
  1432.6 12.3 convolution_convert_fusion.1
  1453.9 36.6 %all-reduce.9 = (bf16[1024]{0:T(1024)(128)(2,1)S(1)}, bf16[1024]{0:T(1024)(128)(2,1)S(1)}, bf16[1024]{0:T(1024)(128)(2,1)S(1)}, bf16[1024]{0:T(1024)(128)(2,1)S(...) all-reduce(bf16[1024]{0:T(1024)(128)(2,1)S(1)} %get-tuple-element.3, ...), channel_id=3, replica_groups=mesh['dp'=8,'seq'=4] {'dp'}, use_global_device_ids=true, to_apply=%region_21.22.clone | all-reduce | flops 12288 | bytes 49152
  1501.6 26.6 %reduce-scatter.13.cloned.1.call-done = bf16[128,3072]{1,0:T(8,128)(2,1)} async-done(((bf16[1024,3072]{1,0:T(8,128)(2,1)}), bf16[128,3072]{1,0:T(8,128)(2,1)}) %reduce-scatter.13.cloned.1.call-update) | async-done | bytes 786448
  1530.4 68.5 %reduce-scatter.7.cloned.1.call-done = bf16[128,1024]{1,0:T(8,128)(2,1)} async-done(((bf16[1024,1024]{1,0:T(8,128)(2,1)}), bf16[128,1024]{1,0:T(8,128)(2,1)}) %reduce-scatter.7.cloned.1.call-update) | async-done | bytes 262160 | tf_op jit(solution)/shard_map/reduce_scatter | solution.py:299
  1598.9 151.6 %reduce-scatter.11.cloned.1.call-done = bf16[512,1024]{1,0:T(8,128)(2,1)} async-done(((bf16[4096,1024]{1,0:T(8,128)(2,1)}), bf16[512,1024]{1,0:T(8,128)(2,1)}) %reduce-scatter.11.cloned.1.call-update) | async-done | bytes 1048592 | tf_op jit(solution)/shard_map/reduce_scatter | solution.py:317
  1750.6 152.1 %reduce-scatter.9.cloned.1.call-done = bf16[128,4096]{1,0:T(8,128)(2,1)} async-done(((bf16[1024,4096]{1,0:T(8,128)(2,1)}), bf16[128,4096]{1,0:T(8,128)(2,1)}) %reduce-scatter.9.cloned.1.call-update) | async-done | bytes 1048592 | tf_op jit(solution)/shard_map/reduce_scatter | solution.py:311
  1902.7 9.8 add_add_fusion.4
  1912.6 61.3 %all-reduce.14.cloned.1.call-done = (bf16[128,3072]{0,1:T(8,128)(2,1)}, bf16[128,1024]{1,0:T(8,128)(2,1)}, bf16[128,4096]{1,0:T(8,128)(2,1)}, bf16[512,1024]{1,0:T(8,128)(2,1)}) async-done(((bf16[128,3072]{0,1:T(8,128)(2,1)}, bf16[128,1024]{1,0:T(8,128)(2,1)}, bf16[128,4096]{1,0:T(8,128)(2,1)}, bf16[512,1024]{1,0:T(8,128)(2,1)}), (bf16[128,3072]{0,1:T(8,128)(2,1)}, bf16[128,1024]{1,0:T(8,128)(2,1)}, ...) | async-done | bytes 3145744 | tf_op jit(solution)/shard_map/psum | solution.py:331
  (429 shorter events, 650.9 us)
Async XLA Ops:
  7.2 104.8 %all-gather.14.cloned.1.call-start = ((), (), s32[]{:S(2)}) async-start(), calls=%async_computation.8 | async-start | bytes 7077888 | tf_op jit(solution)/shard_map/all_gather | solution.py:170
  7.9 573.4 %all-gather.16.cloned.1.call-start = ((), (), s32[]{:S(2)}) async-start(), calls=%async_computation.9 | async-start | bytes 2359296 | tf_op jit(solution)/shard_map/all_gather | solution.py:173
  8.7 577.7 %all-gather.18.cloned.1.call-start = ((), (), s32[]{:S(2)}) async-start(), calls=%async_computation.10 | async-start | bytes 9437184 | tf_op jit(solution)/shard_map/all_gather | solution.py:177
  135.9 59.9 %all-to-all-start = ((bf16[768,3,4,256]{3,0,1,2:T(8,128)(2,1)}), bf16[768,3,4,256]{3,0,1,2:T(8,128)(2,1)}, u32[]{:S(2)}, u32[]{:S(2)}) async-start(bf16[768,3,4,256]{3,0,1,2:T(8,128)(2,1)} %copy.96), calls=%async_computation | async-start | bytes 9437184 | tf_op jit(solution)/shard_map/all_to_all | solution.py:200
  141.1 484.7 %all-gather.20.cloned.1.call-start = ((), (), s32[]{:S(2)}) async-start(), calls=%async_computation.11 | async-start | bytes 9437184 | tf_op jit(solution)/shard_map/all_gather | solution.py:179
  394.0 28.4 %copy-start.1 = (bf16[3072,4,64]{0,2,1:T(8,128)(2,1)}, bf16[3072,4,64]{0,2,1:T(8,128)(2,1)S(1)}, u32[]{:S(2)}) copy-start(bf16[3072,4,64]{0,2,1:T(8,128)(2,1)S(1)} %get-tuple-element.634) | copy-start | bytes 4718596
  394.0 28.4 %copy-start.14 = (f32[1,3072]{1,0:T(1,128)}, f32[1,3072]{1,0:T(1,128)S(1)}, u32[]{:S(2)}) copy-start(f32[1,3072]{1,0:T(1,128)S(1)} %get-tuple-element.653) | copy-start | bytes 36868
  394.0 28.4 %copy-start.21 = (f32[6,4,512]{2,1,0:T(4,128)}, f32[6,4,512]{2,1,0:T(4,128)S(1)}, u32[]{:S(2)}) copy-start(f32[6,4,512]{2,1,0:T(4,128)S(1)} %get-tuple-element.586) | copy-start | bytes 147460
  422.9 22.9 %copy-start.38 = (bf16[128]{0:T(256)(128)(2,1)S(1)}, bf16[128]{0:T(256)(128)(2,1)}, u32[]{:S(2)}) copy-start(bf16[128]{0:T(256)(128)(2,1)} %param.26) | copy-start | bytes 772
  422.9 40.4 %copy-start.39 = (bf16[128]{0:T(256)(128)(2,1)S(1)}, bf16[128]{0:T(256)(128)(2,1)}, u32[]{:S(2)}) copy-start(bf16[128]{0:T(256)(128)(2,1)} %param.27) | copy-start | bytes 772
  422.9 57.3 %copy-start.40 = (bf16[128]{0:T(256)(128)(2,1)S(1)}, bf16[128]{0:T(256)(128)(2,1)}, u32[]{:S(2)}) copy-start(bf16[128]{0:T(256)(128)(2,1)} %param.28) | copy-start | bytes 772
  422.9 74.8 %copy-start.37 = (bf16[512]{0:T(512)(128)(2,1)S(1)}, bf16[512]{0:T(512)(128)(2,1)}, u32[]{:S(2)}) copy-start(bf16[512]{0:T(512)(128)(2,1)} %param.30) | copy-start | bytes 3076
  422.9 100.8 %copy-start.41 = (bf16[128]{0:T(256)(128)(2,1)S(1)}, bf16[128]{0:T(256)(128)(2,1)}, u32[]{:S(2)}) copy-start(bf16[128]{0:T(256)(128)(2,1)} %param.32) | copy-start | bytes 772
  423.0 117.0 %copy-start.42 = (bf16[128]{0:T(256)(128)(2,1)S(1)}, bf16[128]{0:T(256)(128)(2,1)}, u32[]{:S(2)}) copy-start(bf16[128]{0:T(256)(128)(2,1)} %param.33) | copy-start | bytes 772
  423.0 135.1 %copy-start.43 = (bf16[128]{0:T(256)(128)(2,1)S(1)}, bf16[128]{0:T(256)(128)(2,1)}, u32[]{:S(2)}) copy-start(bf16[128]{0:T(256)(128)(2,1)} %param.34) | copy-start | bytes 772
  441.5 132.8 %all-to-all-start.1 = ((bf16[4,2,98304]{2,1,0:T(2,128)(2,1)}), bf16[4,2,98304]{2,1,0:T(2,128)(2,1)}, u32[]{:S(2)}, u32[]{:S(2)}) async-start(bf16[4,2,98304]{2,1,0:T(2,128)(2,1)} %reshape.259), calls=%async_computation.1 | async-start | bytes 3145728 | tf_op jit(solution)/shard_map/all_to_all | solution.py:207
  480.2 197.7 %copy-start.24 = (f32[8,1,128]{2,1,0:T(1,128)}, f32[8,1,128]{2,1,0:T(1,128)S(1)}, u32[]{:S(2)}) copy-start(f32[8,1,128]{2,1,0:T(1,128)S(1)} %convert_element_type.240) | copy-start | bytes 12292
  497.7 128.1 %copy-start.32 = (f32[8,1,128]{2,1,0:T(1,128)}, f32[8,1,128]{2,1,0:T(1,128)S(1)}, u32[]{:S(2)}) copy-start(f32[8,1,128]{2,1,0:T(1,128)S(1)} %convert_element_type.241) | copy-start | bytes 12292
  585.9 92.1 %copy-start.8 = (f32[768,1024]{1,0:T(8,128)}, f32[768,1024]{1,0:T(8,128)S(1)}, u32[]{:S(2)}) copy-start(f32[768,1024]{1,0:T(8,128)S(1)} %get-tuple-element.410) | copy-start | bytes 9437188
  585.9 92.1 %copy-start.19 = (f32[768]{0:T(1024)}, f32[768]{0:T(1024)S(1)}, u32[]{:S(2)}) copy-start(f32[768]{0:T(1024)S(1)} %broadcast_multiply_fusion.1) | copy-start | bytes 9220
  586.4 91.6 %copy-start.26 = (f32[768]{0:T(1024)}, f32[768]{0:T(1024)S(1)}, u32[]{:S(2)}) copy-start(f32[768]{0:T(1024)S(1)} %fusion.94) | copy-start | bytes 9220
  625.8 12.2 copy-start.6
  642.8 21.7 %copy-start.28 = (f32[768]{0:T(1024)}, f32[768]{0:T(1024)S(1)}, u32[]{:S(2)}) copy-start(f32[768]{0:T(1024)S(1)} %negate_multiply_fusion.2) | copy-start | bytes 9220
  684.1 23.6 %all-to-all-start.2 = ((bf16[768,4,256]{0,2,1:T(8,128)(2,1)}), bf16[768,4,256]{0,2,1:T(8,128)(2,1)S(1)}, u32[]{:S(2)}, u32[]{:S(2)}) async-start(bf16[768,4,256]{0,2,1:T(8,128)(2,1)} %bitcast.33), calls=%async_computation.2 | async-start | bytes 3145728 | tf_op jit(solution)/shard_map/all_to_all | solution.py:246
  687.7 840.5 %reduce-scatter.13.cloned.1.call-start = ((), (), s32[]{:S(2)}) async-start(), calls=%async_computation.15 | async-start | bytes 7077888
  707.7 9.8 copy-start.2
  707.8 9.8 copy-start.15
  778.8 15.6 slice-start.3
  782.7 11.7 slice-start.4
  871.9 15.6 slice-start.3
  875.8 11.7 slice-start.4
  897.1 8.8 copy-start.3
  966.8 15.6 slice-start.3
  970.7 11.7 slice-start.4
  992.0 8.8 copy-start.3
  1061.8 15.6 slice-start.3
  1065.7 11.7 slice-start.4
  1087.1 8.8 copy-start.3
  1156.8 15.6 slice-start.3
  1160.7 11.7 slice-start.4
  1182.0 8.8 copy-start.3
  1251.8 15.6 slice-start.3
  1255.7 11.7 slice-start.4
  1411.6 187.3 %reduce-scatter.7.cloned.1.call-start = ((), (), s32[]{:S(2)}) async-start(), calls=%async_computation.12 | async-start | bytes 2359296 | tf_op jit(solution)/shard_map/reduce_scatter | solution.py:299
  1418.0 332.5 %reduce-scatter.11.cloned.1.call-start = ((), (), s32[]{:S(2)}) async-start(), calls=%async_computation.14 | async-start | bytes 9437184 | tf_op jit(solution)/shard_map/reduce_scatter | solution.py:317
  1430.6 472.1 %reduce-scatter.9.cloned.1.call-start = ((), (), s32[]{:S(2)}) async-start(), calls=%async_computation.13 | async-start | bytes 9437184 | tf_op jit(solution)/shard_map/reduce_scatter | solution.py:311
  1444.9 529.0 %all-reduce.14.cloned.1.call-start = ((), (), s32[]{:S(2)}) async-start(), calls=%async_computation.16 | async-start | bytes 6291456 | tf_op jit(solution)/shard_map/psum | solution.py:331
  1451.3 451.4 %copy-start.12 = (f32[768,1024]{1,0:T(8,128)S(1)}, f32[768,1024]{1,0:T(8,128)}, u32[]{:S(2)}) copy-start(f32[768,1024]{1,0:T(8,128)} %copy-done.10) | copy-start | bytes 9437188
  (57 other events, 305.0 us)
Sparse Core Ops, SparseCore 0:
  10.2 101.7 all-gather.13
  114.1 47.4 all-gather.15
  163.8 123.4 all-gather.17
  289.2 123.1 all-gather.19
  1411.7 116.4 reduce-scatter.12
  1532.1 66.7 reduce-scatter.6
  1602.5 147.9 reduce-scatter.10
  1754.6 148.0 reduce-scatter.8
  1905.9 67.9 all-reduce.13
where the time goes:
time: 2000 us; the launch traced here: 1990 us
  matrix products  711 us (36%)
  waiting for transfers between devices  546 us (27%)
  blocking collectives  339 us (17%)
  other arithmetic  225 us (11%)
  local copies, waits for them, and re-layouts  137 us (7%)
    dot_general x24, matrix products, one_block(): jnp.einsum('bhe,lhe->hbl', query_blk[:, part], keys_all[:, part], preferr...  181 us
    dot_general x12, matrix products, one_block(): jnp.einsum('bhe,lhe->hbl', grad_blk[:, part], values_all[:, part], prefer...  167 us
    reduce_scatter x1, waiting for transfers between devices, local(): lax.psum_scatter(local_grads[7].astype(jnp.bfloat16), 'dp', scatter_dimen...  152 us
    reduce_scatter x1, waiting for transfers between devices, local(): lax.psum_scatter(local_grads[9].astype(jnp.bfloat16), 'dp', scatter_dimen...  152 us
    convert_element_type x6, other arithmetic, one_block(): d_scores = (probs_full * (d_probs - row_dot)).astype(jnp.bfloat16)  107 us
    all_to_all x1, blocking collectives, local(): lax.all_to_all(d_heads, 'seq', split_axis=0, concat_axis=2, tiled=True)  74.6 us
    reduce_scatter x1, waiting for transfers between devices, local(): lax.psum_scatter(local_grads[3].astype(jnp.bfloat16), 'dp', scatter_dimen...  68.5 us
    dot_general x12, matrix products, one_block(): jnp.einsum('hbl,lhe->bhe', probs_low, values_all[:, part], preferred_elem...  66.6 us
  transfers between devices with their start and end apart: 12, of which 7 were waited for; matrix products, arithmetic and copies ran while one was open for 19% of the time, Pallas kernels for 0%

commit v1 on v0

--- a/solution.py
+++ b/solution.py
@@ -1,3 +1,4 @@
+import functools
 import jax
 import jax.numpy as jnp
 from jax import lax
@@ -5,6 +6,26 @@
 
 HEAD_DIM = 64
 norm_eps = 1e-05
+
+
+def check_joints_in(load, axis_name, array_dim):
+    piece_now = jax.lax.axis_size(axis_name)
+    v1, local_now = (piece_now, jax.lax.axis_index(axis_name))
+    q_next, a_now = (load, 1)
+    while a_now < v1:
+        f_next = jax.lax.ppermute(
+            q_next,
+            axis_name=axis_name,
+            perm=list(map(lambda tick: (tick, tick ^ a_now), range(v1))),
+        )
+        lower = jnp.concatenate([q_next, f_next], axis=array_dim)
+        mixed_arr = jnp.concatenate([f_next, q_next], axis=array_dim)
+        q_next = jnp.where(local_now & a_now == 0, lower, mixed_arr)
+        a_now = 2 * a_now
+    return q_next
+
+
+unite_core = functools.partial(check_joints_in, axis_name="seq", array_dim=1)
 
 
 def shortened(array):
@@ -202,7 +223,7 @@
     queries = heads_in[:, 0, 0].reshape(length, heads_loc, HEAD_DIM)
     keys_all = heads_in[:, 1, 0].reshape(length, heads_loc, HEAD_DIM)
     values_all = heads_in[:, 2, 0].reshape(length, heads_loc, HEAD_DIM)
-    bias_row = lax.all_gather(key_bias, "seq", axis=1, tiled=True)[0]
+    bias_row = unite_core(key_bias)[0]
     context_heads, log_total = attend_forward(queries, keys_all, values_all, bias_row, score_scale)
     context = lax.all_to_all(
         shortened(context_heads.reshape(length, 1, group_width)),

time: 2000 us -> 2000 us (level)
  blocking collectives: 339 us -> 284 us
  waiting for transfers between devices: 546 us -> 598 us
    all_gather x1 -> x0, blocking collectives: 54.1 us -> none  [local(): bias_row = lax.all_gather(key_bias, 'seq', axis=1, tiled=True)[0]]
    ppermute x0 -> x2, waiting for transfers between devices: none -> 51.5 us  [check_joints_in(): jax.lax.ppermute(q_next, axis_name=axis_name, perm=list(map(lambda tick:...]
  transfers between devices with their start and end apart: 12 -> 14, of which waited for: 7 -> 9; matrix products, arithmetic and copies ran while one was open for 19% -> 19% of each run, Pallas kernels for 0% -> 0%
where the time goes in v1:
time: 2000 us; the launch traced here: 1990 us
  matrix products  711 us (36%)
  waiting for transfers between devices  598 us (30%)
  blocking collectives  284 us (14%)
  other arithmetic  225 us (11%)
  local copies, waits for them, and re-layouts  137 us (7%)
    dot_general x24, matrix products, one_block(): jnp.einsum('bhe,lhe->hbl', query_blk[:, part], keys_all[:, part], preferr...  181 us
    dot_general x12, matrix products, one_block(): jnp.einsum('bhe,lhe->hbl', grad_blk[:, part], values_all[:, part], prefer...  167 us
    reduce_scatter x1, waiting for transfers between devices, local(): lax.psum_scatter(local_grads[7].astype(jnp.bfloat16), 'dp', scatter_dimen...  152 us
    reduce_scatter x1, waiting for transfers between devices, local(): lax.psum_scatter(local_grads[9].astype(jnp.bfloat16), 'dp', scatter_dimen...  152 us
    convert_element_type x6, other arithmetic, one_block(): d_scores = (probs_full * (d_probs - row_dot)).astype(jnp.bfloat16)  107 us
    all_to_all x1, blocking collectives, local(): lax.all_to_all(d_heads, 'seq', split_axis=0, concat_axis=2, tiled=True)  74.6 us
    reduce_scatter x1, waiting for transfers between devices, local(): lax.psum_scatter(local_grads[3].astype(jnp.bfloat16), 'dp', scatter_dimen...  68.6 us
    dot_general x12, matrix products, one_block(): jnp.einsum('hbl,lhe->bhe', probs_low, values_all[:, part], preferred_elem...  66.4 us
  transfers between devices with their start and end apart: 14, of which 9 were waited for; matrix products, arithmetic and copies ran while one was open for 19% of the time, Pallas kernels for 0%

profile of v1, /device:TPU:0, one launch (start us, length us, event | category | flops | bytes accessed | tf_op | source)
XLA Modules:
  0.0 1988.4 jit_solution(7033304393348913157)
XLA Ops:
  9.4 22.5 %all-gather.1 = bf16[8,1,128]{2,1,0:T(2,128)(2,1)S(1)} all-gather(bf16[1,1,128]{2,1,0:T(2,128)(2,1)} %bitcast.231), channel_id=1, replica_groups=mesh['dp'=8,'seq'=4] {'dp'}, dimensions={0}, use_global_device_ids=true | all-gather | bytes 2304 | tf_op jit(solution)/shard_map/all_gather | solution.py:193
  31.9 16.7 all-gather
  48.6 63.4 %all-gather.14.cloned.1.call-done = bf16[1024,3072]{1,0:T(8,128)(2,1)} async-done(((bf16[128,3072]{1,0:T(8,128)(2,1)}), bf16[1024,3072]{1,0:T(8,128)(2,1)}) %all-gather.14.cloned.1.call-update) | async-done | bytes 6291472 | tf_op jit(solution)/shard_map/all_gather | solution.py:191
  112.0 9.0 add_convert_fusion
  121.0 9.6 reshape.383
  145.6 49.3 %collective-permute-done.1 = f32[1,1536]{1,0:T(1,128)S(1)} collective-permute-done((f32[1,1536]{1,0:T(1,128)S(1)}, f32[1,1536]{1,0:T(1,128)S(1)}, u32[]{:S(2)}, u32[]{:S(2)}) %collective-permute-start.1) | collective-permute-done | bytes 6176 | tf_op jit(solution)/shard_map/ppermute | solution.py:16
  212.5 180.4 %while.27 = (s32[]{:T(128)}, bf16[6,512,4,64]{1,3,2,0:T(8,128)(2,1)}, f32[6,4,512]{2,1,0:T(4,128)S(1)}, bf16[6,512,4,64]{1,3,2,0:T(8,128)(2,1)}, bf16[3072,4,64]...) while((s32[]{:T(128)}, bf16[6,512,4,64]{1,3,2,0:T(8,128)(2,1)}, ...), condition=%wide.region_5.6_spmd, body=%wide.region_0.5_spmd.sunk | while | flops 1686765568 | bytes 80098904 | solution.py:102
  398.6 22.8 %reshape.414 = bf16[3072,1,256]{2,1,0:T(2,128)(2,1)} reshape(bf16[6,512,4,64]{3,2,1,0:T(4,128)(2,1)} %copy.114) | data formatting | bytes 3145728 | tf_op jit(solution)/shard_map/reshape;reshape | solution.py:229
  421.9 16.7 reduce.5
  444.8 17.5 all-gather.2
  462.3 16.8 all-gather.3
  479.2 17.5 all-gather.4
  496.7 26.0 %all-gather.5 = bf16[8,1,512]{2,1,0:T(2,128)(2,1)S(1)} all-gather(bf16[1,1,512]{2,1,0:T(2,128)(2,1)S(1)} %reshape.397), channel_id=1, replica_groups=mesh['dp'=8,'seq'=4] {'dp'}, dimensions={0}, use_global_device_ids=true | all-gather | bytes 9216 | tf_op jit(solution)/shard_map/all_gather | solution.py:199
  522.7 16.2 all-gather.6
  538.9 18.2 all-gather.7
  557.1 16.2 all-gather.8
  585.4 39.4 %multiply_convert_fusion.2 = (bf16[768,4096]{1,0:T(8,128)(2,1)}, f32[768,4096]{1,0:T(8,128)}, f32[768,4096]{1,0:T(8,128)}) fusion(f32[4096]{0:T(1024)S(1)} %bitcast.222, bf16[1024,4096]{1,0:T(8,128)(2,1)} %all-gather.18.cloned.1.call-done, f32[768,1024]{1,0:T(8,128)S(1)} %get-tuple-element.410, f32[1024]{0:T(1024)S(1)} %bitcast.226, ...), kind=kOutput, calls=%fused_computation.100 | convolution fusion | flops 6654001152 | bytes 43022336 | tf_op jit(solution)/shard_map/dot_general | solution.py:51
  624.8 11.7 fusion.105
  641.8 21.7 %fusion.106 = (bf16[4096]{0:T(1024)(128)(2,1)}, bf16[768,4096]{1,0:T(8,128)(2,1)}) fusion(f32[768,4096]{1,0:T(8,128)} %get-tuple-element.392, bf16[4096,1024]{1,0:T(8,128)(2,1)} %all-gather.20.cloned.1.call-done, f32[768,1024]{1,0:T(8,128)} %get-tuple-element.390, f32[768]{0:T(1024)S(1)} %negate_multiply_fusion.2, f32[768,4096]{1,0:T(8,128)} %get-tuple-element.411, ...), kind=kOutput, calls=%fused_computation.170 | convolution fusion | flops 6494351360 | bytes 43019264 | tf_op jit(solution)/shard_map/dot_general | solution.py:61
  663.5 13.4 multiply_reduce_fusion.2
  686.7 20.0 %all-to-all-done.2 = bf16[768,4,256]{0,2,1:T(8,128)(2,1)S(1)} async-done(((bf16[768,4,256]{0,2,1:T(8,128)(2,1)}), bf16[768,4,256]{0,2,1:T(8,128)(2,1)S(1)}, u32[]{:S(2)}, u32[]{:S(2)}) %all-to-all-start.2) | async-done | bytes 1572896 | tf_op jit(solution)/shard_map/all_to_all | solution.py:267
  716.5 569.3 %while.28 = (s32[]{:T(128)}, f32[3072,4,64]{0,2,1:T(8,128)}, f32[3072,4,64]{0,2,1:T(8,128)}, bf16[6,512,4,64]{1,3,2,0:T(8,128)(2,1)}, bf16[6,512,4,64]{1,3,2,0:T...) while((s32[]{:T(128)}, f32[3072,4,64]{0,2,1:T(8,128)}, ...), condition=%wide.region_17.18_spmd.clone, body=%wide.region_14.17_spmd.clone.sunk | while | flops 4127193088 | bytes 341160832 | solution.py:165
  739.7 20.2 %multiply_reduce_fusion.7 = (f32[2,512]{1,0:T(2,128)S(1)}, f32[2,512]{1,0:T(2,128)S(1)}, f32[2,512,3072]{2,1,0:T(8,128)}) fusion(f32[2,512,3072]{2,1,0:T(8,128)} %fusion.191, f32[2,512]{1,0:T(2,128)S(1)} %get-tuple-element.546, f32[3072]{0:T(1024)S(1)} %bitcast.204, f32[2,512,3072]{2,1,0:T(8,128)} %fusion.192, f32[2,512]{1,0:T(2,128)S(1)} %get-tuple-element.547, ...), kind=kOutput, calls=%fused_computation.39.clone.1 | convolution fusion | flops 434108416 | bytes 51409408 | tf_op jit(solution)/shard_map/while/body/eval_jaxpr/bhe,lhe->hbl/dot_general | solution.py:132
  759.9 17.9 multiply_convert_fusion.4
  833.0 20.1 %multiply_reduce_fusion.7 = (f32[2,512]{1,0:T(2,128)S(1)}, f32[2,512]{1,0:T(2,128)S(1)}, f32[2,512,3072]{2,1,0:T(8,128)}) fusion(f32[2,512,3072]{2,1,0:T(8,128)} %fusion.191, f32[2,512]{1,0:T(2,128)S(1)} %get-tuple-element.546, f32[3072]{0:T(1024)S(1)} %bitcast.204, f32[2,512,3072]{2,1,0:T(8,128)} %fusion.192, f32[2,512]{1,0:T(2,128)S(1)} %get-tuple-element.547, ...), kind=kOutput, calls=%fused_computation.39.clone.1 | convolution fusion | flops 434108416 | bytes 51409408 | tf_op jit(solution)/shard_map/while/body/eval_jaxpr/bhe,lhe->hbl/dot_general | solution.py:132
  853.1 17.9 multiply_convert_fusion.4
  896.2 8.8 maximum_add_fusion.3
  928.0 20.2 %multiply_reduce_fusion.7 = (f32[2,512]{1,0:T(2,128)S(1)}, f32[2,512]{1,0:T(2,128)S(1)}, f32[2,512,3072]{2,1,0:T(8,128)}) fusion(f32[2,512,3072]{2,1,0:T(8,128)} %fusion.191, f32[2,512]{1,0:T(2,128)S(1)} %get-tuple-element.546, f32[3072]{0:T(1024)S(1)} %bitcast.204, f32[2,512,3072]{2,1,0:T(8,128)} %fusion.192, f32[2,512]{1,0:T(2,128)S(1)} %get-tuple-element.547, ...), kind=kOutput, calls=%fused_computation.39.clone.1 | convolution fusion | flops 434108416 | bytes 51409408 | tf_op jit(solution)/shard_map/while/body/eval_jaxpr/bhe,lhe->hbl/dot_general | solution.py:132
  948.2 17.9 multiply_convert_fusion.4
  991.4 8.8 maximum_add_fusion.3
  1023.2 20.2 %multiply_reduce_fusion.7 = (f32[2,512]{1,0:T(2,128)S(1)}, f32[2,512]{1,0:T(2,128)S(1)}, f32[2,512,3072]{2,1,0:T(8,128)}) fusion(f32[2,512,3072]{2,1,0:T(8,128)} %fusion.191, f32[2,512]{1,0:T(2,128)S(1)} %get-tuple-element.546, f32[3072]{0:T(1024)S(1)} %bitcast.204, f32[2,512,3072]{2,1,0:T(8,128)} %fusion.192, f32[2,512]{1,0:T(2,128)S(1)} %get-tuple-element.547, ...), kind=kOutput, calls=%fused_computation.39.clone.1 | convolution fusion | flops 434108416 | bytes 51409408 | tf_op jit(solution)/shard_map/while/body/eval_jaxpr/bhe,lhe->hbl/dot_general | solution.py:132
  1043.4 17.9 multiply_convert_fusion.4
  1118.3 20.2 %multiply_reduce_fusion.7 = (f32[2,512]{1,0:T(2,128)S(1)}, f32[2,512]{1,0:T(2,128)S(1)}, f32[2,512,3072]{2,1,0:T(8,128)}) fusion(f32[2,512,3072]{2,1,0:T(8,128)} %fusion.191, f32[2,512]{1,0:T(2,128)S(1)} %get-tuple-element.546, f32[3072]{0:T(1024)S(1)} %bitcast.204, f32[2,512,3072]{2,1,0:T(8,128)} %fusion.192, f32[2,512]{1,0:T(2,128)S(1)} %get-tuple-element.547, ...), kind=kOutput, calls=%fused_computation.39.clone.1 | convolution fusion | flops 434108416 | bytes 51409408 | tf_op jit(solution)/shard_map/while/body/eval_jaxpr/bhe,lhe->hbl/dot_general | solution.py:132
  1138.5 17.9 multiply_convert_fusion.4
  1213.4 20.2 %multiply_reduce_fusion.7 = (f32[2,512]{1,0:T(2,128)S(1)}, f32[2,512]{1,0:T(2,128)S(1)}, f32[2,512,3072]{2,1,0:T(8,128)}) fusion(f32[2,512,3072]{2,1,0:T(8,128)} %fusion.191, f32[2,512]{1,0:T(2,128)S(1)} %get-tuple-element.546, f32[3072]{0:T(1024)S(1)} %bitcast.204, f32[2,512,3072]{2,1,0:T(8,128)} %fusion.192, f32[2,512]{1,0:T(2,128)S(1)} %get-tuple-element.547, ...), kind=kOutput, calls=%fused_computation.39.clone.1 | convolution fusion | flops 434108416 | bytes 51409408 | tf_op jit(solution)/shard_map/while/body/eval_jaxpr/bhe,lhe->hbl/dot_general | solution.py:132
  1233.6 17.9 multiply_convert_fusion.4
  1298.8 10.1 copy.110
  1309.0 74.6 %all_to_all.63 = bf16[3072,3,1,256]{3,1,2,0:T(4,128)(2,1)S(1)} all-to-all(bf16[3072,3,1,256]{3,1,2,0:T(4,128)(2,1)} %copy.110), channel_id=1, replica_groups=mesh['dp'=8,'seq'=4] {'seq'}, dimensions={0} | all-to-all | bytes 9437184 | tf_op jit(solution)/shard_map/all_to_all | solution.py:288
  1393.2 9.4 convert_bitcast_fusion
  1417.8 12.5 convolution_convert_fusion
  1432.2 12.3 convolution_convert_fusion.1
  1453.6 36.6 %all-reduce.9 = (bf16[1024]{0:T(1024)(128)(2,1)S(1)}, bf16[1024]{0:T(1024)(128)(2,1)S(1)}, bf16[1024]{0:T(1024)(128)(2,1)S(1)}, bf16[1024]{0:T(1024)(128)(2,1)S(...) all-reduce(bf16[1024]{0:T(1024)(128)(2,1)S(1)} %get-tuple-element.3, ...), channel_id=3, replica_groups=mesh['dp'=8,'seq'=4] {'dp'}, use_global_device_ids=true, to_apply=%region_21.22.clone | all-reduce | flops 12288 | bytes 49152
  1501.2 26.6 %reduce-scatter.13.cloned.1.call-done = bf16[128,3072]{1,0:T(8,128)(2,1)} async-done(((bf16[1024,3072]{1,0:T(8,128)(2,1)}), bf16[128,3072]{1,0:T(8,128)(2,1)}) %reduce-scatter.13.cloned.1.call-update) | async-done | bytes 786448
  1530.1 68.6 %reduce-scatter.7.cloned.1.call-done = bf16[128,1024]{1,0:T(8,128)(2,1)} async-done(((bf16[1024,1024]{1,0:T(8,128)(2,1)}), bf16[128,1024]{1,0:T(8,128)(2,1)}) %reduce-scatter.7.cloned.1.call-update) | async-done | bytes 262160 | tf_op jit(solution)/shard_map/reduce_scatter | solution.py:320
  1598.7 151.7 %reduce-scatter.11.cloned.1.call-done = bf16[512,1024]{1,0:T(8,128)(2,1)} async-done(((bf16[4096,1024]{1,0:T(8,128)(2,1)}), bf16[512,1024]{1,0:T(8,128)(2,1)}) %reduce-scatter.11.cloned.1.call-update) | async-done | bytes 1048592 | tf_op jit(solution)/shard_map/reduce_scatter | solution.py:338
  1750.5 152.1 %reduce-scatter.9.cloned.1.call-done = bf16[128,4096]{1,0:T(8,128)(2,1)} async-done(((bf16[1024,4096]{1,0:T(8,128)(2,1)}), bf16[128,4096]{1,0:T(8,128)(2,1)}) %reduce-scatter.9.cloned.1.call-update) | async-done | bytes 1048592 | tf_op jit(solution)/shard_map/reduce_scatter | solution.py:332
  1902.6 9.8 add_add_fusion.4
  1912.5 61.3 %all-reduce.14.cloned.1.call-done = (bf16[128,3072]{0,1:T(8,128)(2,1)}, bf16[128,1024]{1,0:T(8,128)(2,1)}, bf16[128,4096]{1,0:T(8,128)(2,1)}, bf16[512,1024]{1,0:T(8,128)(2,1)}) async-done(((bf16[128,3072]{0,1:T(8,128)(2,1)}, bf16[128,1024]{1,0:T(8,128)(2,1)}, bf16[128,4096]{1,0:T(8,128)(2,1)}, bf16[512,1024]{1,0:T(8,128)(2,1)}), (bf16[128,3072]{0,1:T(8,128)(2,1)}, bf16[128,1024]{1,0:T(8,128)(2,1)}, ...) | async-done | bytes 3145744 | tf_op jit(solution)/shard_map/psum | solution.py:352
  (438 shorter events, 654.6 us)
Async XLA Ops:
  7.2 104.8 %all-gather.14.cloned.1.call-start = ((), (), s32[]{:S(2)}) async-start(), calls=%async_computation.8 | async-start | bytes 7077888 | tf_op jit(solution)/shard_map/all_gather | solution.py:191
  7.9 572.4 %all-gather.16.cloned.1.call-start = ((), (), s32[]{:S(2)}) async-start(), calls=%async_computation.9 | async-start | bytes 2359296 | tf_op jit(solution)/shard_map/all_gather | solution.py:194
  8.7 576.7 %all-gather.18.cloned.1.call-start = ((), (), s32[]{:S(2)}) async-start(), calls=%async_computation.10 | async-start | bytes 9437184 | tf_op jit(solution)/shard_map/all_gather | solution.py:198
  135.9 59.1 %all-to-all-start = ((bf16[768,3,4,256]{3,0,1,2:T(8,128)(2,1)}), bf16[768,3,4,256]{3,0,1,2:T(8,128)(2,1)}, u32[]{:S(2)}, u32[]{:S(2)}) async-start(bf16[768,3,4,256]{3,0,1,2:T(8,128)(2,1)} %copy.96), calls=%async_computation | async-start | bytes 9437184 | tf_op jit(solution)/shard_map/all_to_all | solution.py:221
  141.1 483.7 %all-gather.20.cloned.1.call-start = ((), (), s32[]{:S(2)}) async-start(), calls=%async_computation.11 | async-start | bytes 9437184 | tf_op jit(solution)/shard_map/all_gather | solution.py:200
  141.1 2.7 collective-permute-start
  143.9 51.1 %collective-permute-start.1 = (f32[1,1536]{1,0:T(1,128)S(1)}, f32[1,1536]{1,0:T(1,128)S(1)}, u32[]{:S(2)}, u32[]{:S(2)}) collective-permute-start(f32[1,1536]{1,0:T(1,128)S(1)} %broadcast_select_fusion.1), channel_id=1, source_target_pairs={{0,2},{1,3},{2,0},{3,1},{4,6},{5,7},{6,4},{7,5},{8,10},{9,11},{10,... | collective-permute-start | bytes 18440 | tf_op jit(solution)/shard_map/ppermute | solution.py:16
  392.9 28.4 %copy-start.1 = (bf16[3072,4,64]{0,2,1:T(8,128)(2,1)}, bf16[3072,4,64]{0,2,1:T(8,128)(2,1)S(1)}, u32[]{:S(2)}) copy-start(bf16[3072,4,64]{0,2,1:T(8,128)(2,1)S(1)} %get-tuple-element.634) | copy-start | bytes 4718596
  392.9 28.4 %copy-start.14 = (f32[1,3072]{1,0:T(1,128)}, f32[1,3072]{1,0:T(1,128)S(1)}, u32[]{:S(2)}) copy-start(f32[1,3072]{1,0:T(1,128)S(1)} %get-tuple-element.653) | copy-start | bytes 36868
  392.9 28.4 %copy-start.21 = (f32[6,4,512]{2,1,0:T(4,128)}, f32[6,4,512]{2,1,0:T(4,128)S(1)}, u32[]{:S(2)}) copy-start(f32[6,4,512]{2,1,0:T(4,128)S(1)} %get-tuple-element.586) | copy-start | bytes 147460
  421.9 22.9 %copy-start.38 = (bf16[128]{0:T(256)(128)(2,1)S(1)}, bf16[128]{0:T(256)(128)(2,1)}, u32[]{:S(2)}) copy-start(bf16[128]{0:T(256)(128)(2,1)} %param.26) | copy-start | bytes 772
  421.9 40.5 %copy-start.39 = (bf16[128]{0:T(256)(128)(2,1)S(1)}, bf16[128]{0:T(256)(128)(2,1)}, u32[]{:S(2)}) copy-start(bf16[128]{0:T(256)(128)(2,1)} %param.27) | copy-start | bytes 772
  421.9 57.3 %copy-start.40 = (bf16[128]{0:T(256)(128)(2,1)S(1)}, bf16[128]{0:T(256)(128)(2,1)}, u32[]{:S(2)}) copy-start(bf16[128]{0:T(256)(128)(2,1)} %param.28) | copy-start | bytes 772
  421.9 74.8 %copy-start.37 = (bf16[512]{0:T(512)(128)(2,1)S(1)}, bf16[512]{0:T(512)(128)(2,1)}, u32[]{:S(2)}) copy-start(bf16[512]{0:T(512)(128)(2,1)} %param.30) | copy-start | bytes 3076
  421.9 100.9 %copy-start.41 = (bf16[128]{0:T(256)(128)(2,1)S(1)}, bf16[128]{0:T(256)(128)(2,1)}, u32[]{:S(2)}) copy-start(bf16[128]{0:T(256)(128)(2,1)} %param.32) | copy-start | bytes 772
  421.9 117.0 %copy-start.42 = (bf16[128]{0:T(256)(128)(2,1)S(1)}, bf16[128]{0:T(256)(128)(2,1)}, u32[]{:S(2)}) copy-start(bf16[128]{0:T(256)(128)(2,1)} %param.33) | copy-start | bytes 772
  421.9 135.2 %copy-start.43 = (bf16[128]{0:T(256)(128)(2,1)S(1)}, bf16[128]{0:T(256)(128)(2,1)}, u32[]{:S(2)}) copy-start(bf16[128]{0:T(256)(128)(2,1)} %param.34) | copy-start | bytes 772
  440.4 132.8 %all-to-all-start.1 = ((bf16[4,2,98304]{2,1,0:T(2,128)(2,1)}), bf16[4,2,98304]{2,1,0:T(2,128)(2,1)}, u32[]{:S(2)}, u32[]{:S(2)}) async-start(bf16[4,2,98304]{2,1,0:T(2,128)(2,1)} %reshape.429), calls=%async_computation.1 | async-start | bytes 3145728 | tf_op jit(solution)/shard_map/all_to_all | solution.py:228
  479.1 197.8 %copy-start.24 = (f32[8,1,128]{2,1,0:T(1,128)}, f32[8,1,128]{2,1,0:T(1,128)S(1)}, u32[]{:S(2)}) copy-start(f32[8,1,128]{2,1,0:T(1,128)S(1)} %convert_element_type.240) | copy-start | bytes 12292
  496.7 128.1 %copy-start.33 = (f32[8,1,128]{2,1,0:T(1,128)}, f32[8,1,128]{2,1,0:T(1,128)S(1)}, u32[]{:S(2)}) copy-start(f32[8,1,128]{2,1,0:T(1,128)S(1)} %convert_element_type.241) | copy-start | bytes 12292
  584.9 92.1 %copy-start.8 = (f32[768,1024]{1,0:T(8,128)}, f32[768,1024]{1,0:T(8,128)S(1)}, u32[]{:S(2)}) copy-start(f32[768,1024]{1,0:T(8,128)S(1)} %get-tuple-element.410) | copy-start | bytes 9437188
  584.9 92.0 %copy-start.19 = (f32[768]{0:T(1024)}, f32[768]{0:T(1024)S(1)}, u32[]{:S(2)}) copy-start(f32[768]{0:T(1024)S(1)} %broadcast_multiply_fusion.1) | copy-start | bytes 9220
  585.3 91.6 %copy-start.26 = (f32[768]{0:T(1024)}, f32[768]{0:T(1024)S(1)}, u32[]{:S(2)}) copy-start(f32[768]{0:T(1024)S(1)} %fusion.94) | copy-start | bytes 9220
  624.8 12.2 copy-start.6
  641.8 21.7 %copy-start.28 = (f32[768]{0:T(1024)}, f32[768]{0:T(1024)S(1)}, u32[]{:S(2)}) copy-start(f32[768]{0:T(1024)S(1)} %negate_multiply_fusion.2) | copy-start | bytes 9220
  683.0 23.6 %all-to-all-start.2 = ((bf16[768,4,256]{0,2,1:T(8,128)(2,1)}), bf16[768,4,256]{0,2,1:T(8,128)(2,1)S(1)}, u32[]{:S(2)}, u32[]{:S(2)}) async-start(bf16[768,4,256]{0,2,1:T(8,128)(2,1)} %bitcast.33), calls=%async_computation.2 | async-start | bytes 3145728 | tf_op jit(solution)/shard_map/all_to_all | solution.py:267
  686.6 841.2 %reduce-scatter.13.cloned.1.call-start = ((), (), s32[]{:S(2)}) async-start(), calls=%async_computation.15 | async-start | bytes 7077888
  706.7 9.9 copy-start.2
  706.7 9.9 copy-start.15
  777.8 15.6 slice-start.3
  781.7 11.7 slice-start.4
  871.0 15.6 slice-start.3
  874.9 11.7 slice-start.4
  966.1 15.6 slice-start.3
  970.0 11.7 slice-start.4
  1061.3 15.6 slice-start.3
  1065.2 11.7 slice-start.4
  1086.5 8.8 copy-start.3
  1156.4 15.6 slice-start.3
  1160.3 11.7 slice-start.4
  1251.5 15.6 slice-start.3
  1255.4 11.7 slice-start.4
  1276.7 8.8 copy-start.3
  1411.3 187.5 %reduce-scatter.7.cloned.1.call-start = ((), (), s32[]{:S(2)}) async-start(), calls=%async_computation.12 | async-start | bytes 2359296 | tf_op jit(solution)/shard_map/reduce_scatter | solution.py:320
  1417.7 332.7 %reduce-scatter.11.cloned.1.call-start = ((), (), s32[]{:S(2)}) async-start(), calls=%async_computation.14 | async-start | bytes 9437184 | tf_op jit(solution)/shard_map/reduce_scatter | solution.py:338
  1430.3 472.3 %reduce-scatter.9.cloned.1.call-start = ((), (), s32[]{:S(2)}) async-start(), calls=%async_computation.13 | async-start | bytes 9437184 | tf_op jit(solution)/shard_map/reduce_scatter | solution.py:332
  1444.6 529.2 %all-reduce.14.cloned.1.call-start = ((), (), s32[]{:S(2)}) async-start(), calls=%async_computation.16 | async-start | bytes 6291456 | tf_op jit(solution)/shard_map/psum | solution.py:352
  1451.0 451.6 %copy-start.12 = (f32[768,1024]{1,0:T(8,128)S(1)}, f32[768,1024]{1,0:T(8,128)}, u32[]{:S(2)}) copy-start(f32[768,1024]{1,0:T(8,128)} %copy-done.10) | copy-start | bytes 9437188
  (59 other events, 321.7 us)
Sparse Core Ops, SparseCore 0:
  10.2 101.7 all-gather.13
  114.1 47.4 all-gather.15
  163.8 123.4 all-gather.17
  289.2 123.1 all-gather.19
  1411.4 116.3 reduce-scatter.12
  1531.8 66.9 reduce-scatter.6
  1602.4 148.0 reduce-scatter.10
  1754.5 148.0 reduce-scatter.8
  1905.8 67.9 all-reduce.13
